TPU v7x, 128 devices: a whole 4x4x4 slice. The times are simulated.
128 devices in a mesh: corpus: 32 (over z, x, core), replica: 4 (over y).
Axes of the slice: x: 4, y: 4, z: 4, core: 2. Of those that a mesh axis runs over, the one named last changes fastest.
Arguments:
- queries: bfloat16 [1024, 32, 128], P(('corpus', 'replica')), may hold values from -0.5390625 to 0.5390625
- cand_dev: int32 [1024, 16], P(('corpus', 'replica')), may hold values from 0 to 127, all different within a row; in each aligned block of 8 rows (0 to 7, 8 to 15, ...) at most 2 rows name the same one
- cand_slot: int32 [1024, 256], P(('corpus', 'replica')), may hold values from 0 to 511
- codes: int32 [65536, 4096], P(('corpus', 'replica')), may hold values from 0 to 255
- cent_ids: int32 [65536, 128], P(('corpus', 'replica')), may hold values from 0 to 65535
- lengths: int32 [65536], P(('corpus', 'replica')), may hold values from 1 to 128
- centroids: bfloat16 [65536, 128], replicated, may hold values from -0.5390625 to 0.5390625
- buckets: float32 [4], replicated, may hold values from -0.36 to 0.36
Outputs:
- scores: float32 [1024, 256], P(('corpus', 'replica'))
Inputs may be any that keep to these rules, and one draw needn't show every extreme that they name: `cand_dev`: each row names 16 different devices. Among the 8 rows of one device, no device is named more than 2 times, and some device is named exactly 2 times in some or all of these blocks.
All inputs are finite; a program needn't handle non-finite values.
Results may differ from a plain program's by a relative error of at most 0.0003.
Values may be sent and summed in bfloat16 or wider, within the bound.
No kernel may reach another device: no remote copies, remote signals or barrier semaphores. Data moves between devices by JAX's collectives and lax.ppermute only.
A program may use at most 256 MiB of HBM per device.

v0:
```python
import math

import jax
import jax.numpy as jnp
from jax import lax
from jax.sharding import PartitionSpec as P

DIM = 128
PTOK = 128


def unpack(code_rows, cid_rows, centroids, buckets):
    lead = code_rows.shape[:-1]
    words = code_rows.reshape(lead + (PTOK, DIM // 4))
    shifts = 2 * jnp.arange(4, dtype=jnp.int32)
    bits = jnp.bitwise_and(jnp.right_shift(words[..., None], shifts), 3)
    bits = bits.reshape(lead + (PTOK, DIM))
    residual = jnp.zeros(bits.shape, jnp.float32)
    for level in range(4):
        residual = residual + jnp.where(bits == level, buckets[level], jnp.float32(0.0))
    looked = jnp.take(centroids, cid_rows.reshape(-1), axis=0).reshape(lead + (PTOK, DIM))
    embed = looked.astype(jnp.float32) + residual
    embed = embed * lax.rsqrt(jnp.sum(embed * embed, axis=-1, keepdims=True) + 1e-06)
    return embed.astype(jnp.bfloat16)


def select_rows(onehot, values):
    return jnp.dot(
        onehot, values, precision=lax.Precision.HIGHEST, preferred_element_type=jnp.float32
    )


def local(queries, cand_dev, cand_slot, codes, cent_ids, lengths, centroids, buckets):
    devices = lax.axis_size(("corpus", "replica"))
    q_rows, k_top = cand_dev.shape
    per = cand_slot.shape[1] // k_top
    capacity = max(2, 2 * q_rows * k_top // devices)
    tok_feat = queries.shape[1] * queries.shape[2]
    slot_grid = cand_slot.reshape(q_rows, k_top, per)
    hits = (cand_dev[:, :, None] == jnp.arange(devices, dtype=jnp.int32)).astype(jnp.int32)
    per_query = jnp.sum(hits, axis=1)
    before = jnp.cumsum(per_query, axis=0) - per_query
    place = jnp.sum(hits * before[:, None, :], axis=2)
    dest = (cand_dev * capacity + place).reshape(-1)
    route = jnp.arange(devices * capacity, dtype=jnp.int32)[:, None] == dest[None, :]
    live_bias = jnp.where(
        jnp.arange(PTOK, dtype=jnp.int32)[None, :] < lengths[:, None],
        jnp.float32(0.0),
        jnp.float32(-1e30),
    )
    n_pass = codes.shape[0]
    stored = unpack(codes, cent_ids, centroids, buckets).reshape(n_pass, PTOK * DIM)
    spread = jnp.broadcast_to(queries[:, None], (q_rows, k_top) + queries.shape[1:]).reshape(
        q_rows * k_top, tok_feat
    )
    send_q = jnp.dot(route.astype(jnp.bfloat16), spread, preferred_element_type=jnp.float32).astype(
        jnp.bfloat16
    )
    send_q = send_q.reshape((devices, capacity) + queries.shape[1:])
    send_s = select_rows(
        route.astype(jnp.float32), slot_grid.reshape(q_rows * k_top, per).astype(jnp.float32)
    )
    send_s = send_s.astype(jnp.int32).reshape(devices, capacity, per)
    send_q, send_s = (send_q, send_s)
    recv_q = lax.all_to_all(send_q, ("corpus", "replica"), split_axis=0, concat_axis=0, tiled=True)
    recv_s = lax.all_to_all(send_s, ("corpus", "replica"), split_axis=0, concat_axis=0, tiled=True)
    lead = recv_q.shape[:2]
    count = lead[0] * lead[1]
    step = math.gcd(count, 16)
    flat_q = recv_q.reshape((count // step, step) + recv_q.shape[2:])
    flat_s = recv_s.reshape(count // step, step * per)

    def block(items):
        block_q, block_s = items
        embed = jnp.take(stored, block_s, axis=0).reshape(step, per, PTOK, DIM)
        bias = jnp.take(live_bias, block_s, axis=0).reshape(step, 1, per, PTOK)
        sims = jnp.einsum("bqf,bptf->bqpt", block_q, embed, preferred_element_type=jnp.float32)
        best = jnp.max(sims + bias, axis=3)
        return jnp.sum(best, axis=1)

    totals = lax.map(block, (flat_q, flat_s))
    scored = totals.reshape(lead + (per,))
    returned = lax.all_to_all(
        scored, ("corpus", "replica"), split_axis=0, concat_axis=0, tiled=True
    )
    result = select_rows(route.astype(jnp.float32).T, returned.reshape(devices * capacity, per))
    return result.reshape(q_rows, k_top * per)


def solution(mesh):
    in_specs = (
        P(("corpus", "replica"), None, None),
        P(("corpus", "replica"), None),
        P(("corpus", "replica"), None),
        P(("corpus", "replica"), None),
        P(("corpus", "replica"), None),
        P(("corpus", "replica")),
        P(),
        P(),
    )
    out_specs = P(("corpus", "replica"), None)
    return jax.shard_map(local, mesh=mesh, in_specs=in_specs, out_specs=out_specs, check_vma=False)
```

profile of v0, /device:TPU:1, one launch (start us, length us, event | category | flops | bytes accessed | tf_op | source)
XLA Modules:
  0.0 1217.7 jit_solution(11176031324094238850)
XLA Ops:
  4.3 11.5 all-to-all-start.1
  30.4 10.0 copy.43
  46.0 21.5 %copy.61 = s32[16,8,512,128]{3,1,2,0:T(8,128)} copy(s32[16,8,512,128]{3,2,1,0:T(8,128)S(1)} %bitcast.82) | data formatting | bytes 67108864
  67.5 33.4 %copy.45 = s32[65536,128]{1,0:T(8,128)} copy(s32[65536,128]{0,1:T(8,128)} %bitcast.83) | data formatting | bytes 67108864 | tf_op jit(solution)/shard_map/shift_right_arithmetic | solution.py:16
  102.8 225.7 %gather_fusion.2 = bf16[65536,128]{1,0:T(8,128)(2,1)} fusion(bf16[65536,128]{1,0:T(8,128)(2,1)} %param.16, s32[65536]{0:T(1024)S(1)} %broadcast_clamp_fusion), kind=kCustom, calls=%fused_computation.2 | custom fusion | bytes 33816576 | tf_op jit(solution)/shard_map/jit(_take)/gather | solution.py:21
  328.5 10.1 all-to-all-start
  338.7 32.7 %multiply_reduce_fusion = f32[65536]{0:T(1024)S(1)} fusion(s32[65536,128]{1,0:T(8,128)} %copy.45, f32[]{:T(128)} %bitcast.10, f32[]{:T(128)} %bitcast.9, f32[]{:T(128)} %bitcast.8, f32[]{:T(128)} %bitcast.7, s32[128]{0:T(128)S(1)} %shift_right_arithmetic.44, bf16[65536,128]{1,0:T(8,128)(2,1)} %gather_fusion.2, pred[65536]{0:T(1024)(128)(4,1)S(1)} %fusion.22), kind=kLoop, calls=%fused_computation.26 | loop fusion | flops 150929408 | bytes 50659856 | tf_op jit(solution)/shard_map/reduce_sum | solution.py:23
  371.4 25.3 %gather.19 = bf16[512,16384]{1,0:T(8,128)(2,1)} reshape(bf16[65536,128]{1,0:T(8,128)(2,1)} %gather_fusion.2) | data formatting | bytes 33554432 | tf_op jit(solution)/shard_map/jit(_take)/gather | solution.py:21
  396.9 13.6 %shift_right_arithmetic.41.clone = s32[512,128,32,4]{0,3,2,1:T(4,128)} broadcast(s32[512,128,32]{0,2,1:T(8,128)} %bitcast.85), dimensions={0,1,2} | broadcast | bytes 41943040 | tf_op jit(solution)/shard_map/shift_right_arithmetic | solution.py:16
  410.5 38.2 %shift_right_arithmetic.42 = s32[512,16384]{0,1:T(8,128)} reshape(s32[512,128,32,4]{0,3,2,1:T(4,128)} %shift_right_arithmetic.41.clone) | data formatting | bytes 67108864 | tf_op jit(solution)/shard_map/shift_right_arithmetic | solution.py:16
  448.7 22.5 %copy.41 = bf16[512,16384]{0,1:T(8,128)(2,1)} copy(bf16[512,16384]{1,0:T(8,128)(2,1)} %gather.19) | data formatting | bytes 33554432 | tf_op jit(solution)/shard_map/jit(_take)/gather | solution.py:21
  471.4 30.9 %fusion.11 = bf16[512,16384]{0,1:T(8,128)(2,1)} fusion(s32[512,16384]{0,1:T(8,128)} %shift_right_arithmetic.42, bf16[512,16384]{0,1:T(8,128)(2,1)} %copy.41, f32[512,128]{0,1:T(8,128)S(1)} %copy.46, f32[]{:T(128)} %bitcast.10, f32[]{:T(128)} %bitcast.9, f32[]{:T(128)} %bitcast.8, f32[]{:T(128)} %bitcast.7, s32[16384]{0:T(1024)S(1)} %broadcast_bitcast_fusion, ...), kind=kLoop, calls=%fused_computation.25 | loop fusion | flops 150994944 | bytes 67502096 | tf_op jit(solution)/shard_map/convert_element_type | solution.py:24
  502.3 21.3 %copy.47 = bf16[512,16384]{1,0:T(8,128)(2,1)} copy(bf16[512,16384]{0,1:T(8,128)(2,1)} %fusion.11) | data formatting | bytes 33554432
  523.9 672.8 %while.11 = (s32[]{:T(128)}, f32[16,16,16]{2,1,0:T(8,128)S(1)}, bf16[16,16,32,128]{3,2,1,0:T(8,128)(2,1)S(1)}, s32[16,256]{1,0:T(8,128)S(1)}, bf16[512,16384]{1,...) while((s32[]{:T(128)}, f32[16,16,16]{2,1,0:T(8,128)S(1)}, ...), condition=%wide.region_7.8_spmd.clone, body=%wide.region_4.7_spmd.clone.sunk | while | flops 274893824 | bytes 43093608 | solution.py:81
  539.1 24.3 %gather_fusion.1 = bf16[256,16384]{1,0:T(8,128)(2,1)} fusion(bf16[512,16384]{1,0:T(8,128)(2,1)} %get-tuple-element.150, s32[1024]{0:T(1024)S(1)} %pad_clamp_fusion.2), kind=kCustom, calls=%fused_computation.clone.clone.1 | custom fusion | bytes 16778240 | tf_op jit(solution)/shard_map/while/body/eval_jaxpr/jit(_take)/gather | solution.py:75
  580.3 24.3 %gather_fusion.1 = bf16[256,16384]{1,0:T(8,128)(2,1)} fusion(bf16[512,16384]{1,0:T(8,128)(2,1)} %get-tuple-element.150, s32[1024]{0:T(1024)S(1)} %pad_clamp_fusion.2), kind=kCustom, calls=%fused_computation.clone.clone.1 | custom fusion | bytes 16778240 | tf_op jit(solution)/shard_map/while/body/eval_jaxpr/jit(_take)/gather | solution.py:75
  621.5 24.3 %gather_fusion.1 = bf16[256,16384]{1,0:T(8,128)(2,1)} fusion(bf16[512,16384]{1,0:T(8,128)(2,1)} %get-tuple-element.150, s32[1024]{0:T(1024)S(1)} %pad_clamp_fusion.2), kind=kCustom, calls=%fused_computation.clone.clone.1 | custom fusion | bytes 16778240 | tf_op jit(solution)/shard_map/while/body/eval_jaxpr/jit(_take)/gather | solution.py:75
  662.6 24.3 %gather_fusion.1 = bf16[256,16384]{1,0:T(8,128)(2,1)} fusion(bf16[512,16384]{1,0:T(8,128)(2,1)} %get-tuple-element.150, s32[1024]{0:T(1024)S(1)} %pad_clamp_fusion.2), kind=kCustom, calls=%fused_computation.clone.clone.1 | custom fusion | bytes 16778240 | tf_op jit(solution)/shard_map/while/body/eval_jaxpr/jit(_take)/gather | solution.py:75
  703.8 24.3 %gather_fusion.1 = bf16[256,16384]{1,0:T(8,128)(2,1)} fusion(bf16[512,16384]{1,0:T(8,128)(2,1)} %get-tuple-element.150, s32[1024]{0:T(1024)S(1)} %pad_clamp_fusion.2), kind=kCustom, calls=%fused_computation.clone.clone.1 | custom fusion | bytes 16778240 | tf_op jit(solution)/shard_map/while/body/eval_jaxpr/jit(_take)/gather | solution.py:75
  745.0 24.3 %gather_fusion.1 = bf16[256,16384]{1,0:T(8,128)(2,1)} fusion(bf16[512,16384]{1,0:T(8,128)(2,1)} %get-tuple-element.150, s32[1024]{0:T(1024)S(1)} %pad_clamp_fusion.2), kind=kCustom, calls=%fused_computation.clone.clone.1 | custom fusion | bytes 16778240 | tf_op jit(solution)/shard_map/while/body/eval_jaxpr/jit(_take)/gather | solution.py:75
  786.1 24.3 %gather_fusion.1 = bf16[256,16384]{1,0:T(8,128)(2,1)} fusion(bf16[512,16384]{1,0:T(8,128)(2,1)} %get-tuple-element.150, s32[1024]{0:T(1024)S(1)} %pad_clamp_fusion.2), kind=kCustom, calls=%fused_computation.clone.clone.1 | custom fusion | bytes 16778240 | tf_op jit(solution)/shard_map/while/body/eval_jaxpr/jit(_take)/gather | solution.py:75
  827.3 24.3 %gather_fusion.1 = bf16[256,16384]{1,0:T(8,128)(2,1)} fusion(bf16[512,16384]{1,0:T(8,128)(2,1)} %get-tuple-element.150, s32[1024]{0:T(1024)S(1)} %pad_clamp_fusion.2), kind=kCustom, calls=%fused_computation.clone.clone.1 | custom fusion | bytes 16778240 | tf_op jit(solution)/shard_map/while/body/eval_jaxpr/jit(_take)/gather | solution.py:75
  868.5 24.3 %gather_fusion.1 = bf16[256,16384]{1,0:T(8,128)(2,1)} fusion(bf16[512,16384]{1,0:T(8,128)(2,1)} %get-tuple-element.150, s32[1024]{0:T(1024)S(1)} %pad_clamp_fusion.2), kind=kCustom, calls=%fused_computation.clone.clone.1 | custom fusion | bytes 16778240 | tf_op jit(solution)/shard_map/while/body/eval_jaxpr/jit(_take)/gather | solution.py:75
  909.6 24.3 %gather_fusion.1 = bf16[256,16384]{1,0:T(8,128)(2,1)} fusion(bf16[512,16384]{1,0:T(8,128)(2,1)} %get-tuple-element.150, s32[1024]{0:T(1024)S(1)} %pad_clamp_fusion.2), kind=kCustom, calls=%fused_computation.clone.clone.1 | custom fusion | bytes 16778240 | tf_op jit(solution)/shard_map/while/body/eval_jaxpr/jit(_take)/gather | solution.py:75
  950.8 24.3 %gather_fusion.1 = bf16[256,16384]{1,0:T(8,128)(2,1)} fusion(bf16[512,16384]{1,0:T(8,128)(2,1)} %get-tuple-element.150, s32[1024]{0:T(1024)S(1)} %pad_clamp_fusion.2), kind=kCustom, calls=%fused_computation.clone.clone.1 | custom fusion | bytes 16778240 | tf_op jit(solution)/shard_map/while/body/eval_jaxpr/jit(_take)/gather | solution.py:75
  992.0 24.3 %gather_fusion.1 = bf16[256,16384]{1,0:T(8,128)(2,1)} fusion(bf16[512,16384]{1,0:T(8,128)(2,1)} %get-tuple-element.150, s32[1024]{0:T(1024)S(1)} %pad_clamp_fusion.2), kind=kCustom, calls=%fused_computation.clone.clone.1 | custom fusion | bytes 16778240 | tf_op jit(solution)/shard_map/while/body/eval_jaxpr/jit(_take)/gather | solution.py:75
  1033.1 24.3 %gather_fusion.1 = bf16[256,16384]{1,0:T(8,128)(2,1)} fusion(bf16[512,16384]{1,0:T(8,128)(2,1)} %get-tuple-element.150, s32[1024]{0:T(1024)S(1)} %pad_clamp_fusion.2), kind=kCustom, calls=%fused_computation.clone.clone.1 | custom fusion | bytes 16778240 | tf_op jit(solution)/shard_map/while/body/eval_jaxpr/jit(_take)/gather | solution.py:75
  1074.3 24.3 %gather_fusion.1 = bf16[256,16384]{1,0:T(8,128)(2,1)} fusion(bf16[512,16384]{1,0:T(8,128)(2,1)} %get-tuple-element.150, s32[1024]{0:T(1024)S(1)} %pad_clamp_fusion.2), kind=kCustom, calls=%fused_computation.clone.clone.1 | custom fusion | bytes 16778240 | tf_op jit(solution)/shard_map/while/body/eval_jaxpr/jit(_take)/gather | solution.py:75
  1115.5 24.3 %gather_fusion.1 = bf16[256,16384]{1,0:T(8,128)(2,1)} fusion(bf16[512,16384]{1,0:T(8,128)(2,1)} %get-tuple-element.150, s32[1024]{0:T(1024)S(1)} %pad_clamp_fusion.2), kind=kCustom, calls=%fused_computation.clone.clone.1 | custom fusion | bytes 16778240 | tf_op jit(solution)/shard_map/while/body/eval_jaxpr/jit(_take)/gather | solution.py:75
  1139.8 9.2 copy.63
  1156.6 24.3 %gather_fusion.1 = bf16[256,16384]{1,0:T(8,128)(2,1)} fusion(bf16[512,16384]{1,0:T(8,128)(2,1)} %get-tuple-element.150, s32[1024]{0:T(1024)S(1)} %pad_clamp_fusion.2), kind=kCustom, calls=%fused_computation.clone.clone.1 | custom fusion | bytes 16778240 | tf_op jit(solution)/shard_map/while/body/eval_jaxpr/jit(_take)/gather | solution.py:75
  1196.7 19.8 %all_to_all.15 = f32[128,2,16]{2,1,0:T(2,128)S(1)} all-to-all(f32[128,2,16]{2,1,0:T(2,128)S(1)} %bitcast.92), channel_id=1, replica_groups=mesh['corpus'=32,'replica'=4] {'corpus','replica'}, dimensions={0} | all-to-all | bytes 32768 | tf_op jit(solution)/shard_map/all_to_all | solution.py:83
  (232 shorter events, 287.9 us)
Async XLA Ops:
  2.6 43.4 %copy-start.2 = (s32[128]{0:T(128)}, s32[128]{0:T(128)S(1)}, u32[]{:S(2)}) copy-start(s32[128]{0:T(128)S(1)} %eq.84) | copy-start | bytes 1540
  4.3 324.2 %all-to-all-start.1 = ((s32[128,2,16]{2,1,0:T(2,128)}), s32[128,2,16]{2,1,0:T(2,128)S(1)}, u32[]{:S(2)}, u32[]{:S(2)}) async-start(s32[128,2,16]{2,1,0:T(2,128)} %bitcast.1), calls=%async_computation.1 | async-start | bytes 262144 | tf_op jit(solution)/shard_map/all_to_all | solution.py:66
  328.5 195.3 %all-to-all-start = ((bf16[128,2,32,128]{3,2,1,0:T(8,128)(2,1)}), bf16[128,2,32,128]{3,2,1,0:T(8,128)(2,1)S(1)}, u32[]{:S(2)}, u32[]{:S(2)}) async-start(bf16[128,2,32,128]{3,2,1,0:T(8,128)(2,1)} %bitcast.32), calls=%async_computation | async-start | bytes 4194304 | tf_op jit(solution)/shard_map/all_to_all | solution.py:65
  448.7 22.5 %copy-start = (s32[512,128]{1,0:T(8,128)S(1)}, s32[512,128]{1,0:T(8,128)}, u32[]{:S(2)}) copy-start(s32[512,128]{1,0:T(8,128)} %param.14) | copy-start | bytes 786436
  502.3 21.5 %copy-start.1 = (s32[512]{0:T(512)S(1)}, s32[512]{0:T(512)}, u32[]{:S(2)}) copy-start(s32[512]{0:T(512)} %param.15) | copy-start | bytes 6148
  523.8 692.7 %copy-start.3 = (s32[128]{0:T(128)S(1)}, s32[128]{0:T(128)}, u32[]{:S(2)}) copy-start(s32[128]{0:T(128)} %copy-done.2) | copy-start | bytes 1540
where the time goes:
time: 1220 us
  local copies, waits for them, and re-layouts  981 us (80%)
  matrix products  104 us (9%)
  other arithmetic  75.2 us (6%)
  starting transfers between devices  21.6 us (2%)
  blocking collectives  19.8 us (2%)
  loops' own time  15.3 us (1%)
    gather x16, local copies, waits for them, and re-layouts, block(): embed = jnp.take(stored, block_s, axis=0).reshape(step, per, PTOK, DIM)  388 us
    gather x3, local copies, waits for them, and re-layouts, unpack(): jnp.take(centroids, cid_rows.reshape(-1), axis=0)  274 us
    while x16, local copies, waits for them, and re-layouts  147 us
    dot_general x16, matrix products, block(): jnp.einsum('bqf,bptf->bqpt', block_q, embed, preferred_element_type=jnp.f...  103 us
    shift_right_arithmetic x8, local copies, waits for them, and re-layouts, unpack(): bits = jnp.bitwise_and(jnp.right_shift(words[..., None], shifts), 3)  101 us
    unnamed x12, local copies, waits for them, and re-layouts  53.7 us
    reduce_sum x1, other arithmetic, unpack(): jnp.sum(embed * embed, axis=-1, keepdims=True) + 1e-06  32.7 us
    convert_element_type x1, other arithmetic, unpack(): return embed.astype(jnp.bfloat16)  30.9 us
  transfers between devices with their start and end apart: 2, of which 0 were waited for; matrix products, arithmetic and copies ran while one was open for 41% of the time, Pallas kernels for 0%

commit v1 on v0

v1 whole, which is shorter than its diff:
```python
import functools

import jax
import jax.numpy as jnp
from jax import lax
from jax.experimental import pallas as pl
from jax.experimental.pallas import tpu as pltpu
from jax.sharding import PartitionSpec as P

DIM = 128
PTOK = 128
CHUNK = 32
AXES = ("corpus", "replica")

TAB_STEP = 1024
TAB_BUFS = 10
GROUP_BITS = 3
GROUP = 1 << GROUP_BITS
PARTS = 8


def load_table(cent, tab, buf, sem):
    steps = cent.shape[0] // TAB_STEP

    def copy(i, slot):
        start = pl.multiple_of(i * TAB_STEP, TAB_STEP)
        return pltpu.make_async_copy(cent.at[pl.ds(start, TAB_STEP)], buf.at[slot], sem.at[slot])

    for i in range(min(TAB_BUFS - 1, steps)):
        copy(i, i).start()

    def body(i, carry):
        @pl.when(i + TAB_BUFS - 1 < steps)
        def _():
            copy(i + TAB_BUFS - 1, lax.rem(i + TAB_BUFS - 1, TAB_BUFS)).start()

        slot = lax.rem(i, TAB_BUFS)
        copy(i, slot).wait()
        start = pl.multiple_of(i * TAB_STEP, TAB_STEP)
        tab[pl.ds(start, TAB_STEP), :] = buf[slot].astype(jnp.float32)
        return carry

    lax.fori_loop(0, steps, body, 0)


def unpack_kernel(
    items, starts, lefts, lasts, bounds, buckets, ids_hbm, codes_hbm, cent, out,
    tab, buf, ids, codes, stored, centre, words, raws, squares, spread_of, ones,
    sem, ids_sem, codes_sem, out_sem,
):
    n_items = items.shape[0]
    parts = codes_sem.shape[0]
    code_rows = codes.shape[0] // parts
    part_chunks = n_items // parts

    def codes_copy(j):
        at = pl.ds(pl.multiple_of(j * code_rows, code_rows), code_rows)
        return pltpu.make_async_copy(codes_hbm.at[at], codes.at[at], codes_sem.at[j])

    def out_copy(j):
        at = pl.ds(j * part_chunks, part_chunks)
        return pltpu.make_async_copy(stored.at[at], out.at[at], out_sem)

    ids_copy = pltpu.make_async_copy(ids_hbm, ids, ids_sem)
    ids_copy.start()
    codes_copy(0).start()
    lane = lax.broadcasted_iota(jnp.int32, (8, DIM), 1)
    sub = lax.broadcasted_iota(jnp.int32, (8, DIM), 0)
    low_bit = jnp.left_shift(1, 2 * jnp.bitwise_and(lane, 3))
    high_bit = jnp.left_shift(2, 2 * jnp.bitwise_and(lane, 3))
    source = lax.broadcasted_iota(jnp.int32, (DIM, 4 * DIM), 0)
    target = jnp.right_shift(lax.broadcasted_iota(jnp.int32, (DIM, 4 * DIM), 1), 2)
    spread_of[...] = jnp.where(source == target, 1.0, 0.0).astype(jnp.bfloat16)
    ones[...] = jnp.ones_like(ones)
    centre[1] = jnp.zeros_like(centre[1])
    words[1] = jnp.zeros_like(words[1])
    raws[...] = jnp.zeros_like(raws)
    squares[...] = jnp.zeros_like(squares)
    load_table(cent, tab, buf, sem)
    for j in range(1, parts):
        codes_copy(j).start()
    ids_copy.wait()
    b0, b1, b2, b3 = (buckets[i] for i in range(4))

    def gather(group, side):
        code_rows = []
        for n in range(GROUP):
            item = group * GROUP + n
            code = items[item]
            code_rows.append(codes[pl.ds(starts[item], 8, stride=8), :])
            for k in range(4):
                for r in range(8):
                    token = ids.at[pl.ds((4 * r + k) * n_items, n_items)][code]
                    centre[side, pl.ds(CHUNK * n + 8 * k + r, 1), :] = tab[pl.ds(token, 1), :]
        packed = jnp.concatenate(code_rows, axis=0).astype(jnp.float32).astype(jnp.bfloat16)
        words[side] = jnp.dot(packed, spread_of[...], preferred_element_type=jnp.float32)

    def decode(side):
        for n in range(GROUP):
            parts = []
            for k in range(4):
                at = pl.ds(CHUNK * n + 8 * k, 8)
                word = words[side, pl.ds(8 * n, 8), pl.ds(DIM * k, DIM)].astype(jnp.int32)
                low = jnp.bitwise_and(word, low_bit) != 0
                high = jnp.bitwise_and(word, high_bit) != 0
                residual = jnp.where(high, jnp.where(low, b3, b2), jnp.where(low, b1, b0))
                raw = centre[side, at, :] + residual
                raws[side, at, :] = raw
                parts.append(raw * raw)
            for h in range(2):
                square = jnp.concatenate(parts[2 * h : 2 * h + 2], axis=0)
                top = square.astype(jnp.bfloat16)
                rest = (square - top.astype(jnp.float32)).astype(jnp.bfloat16)
                squares[side, pl.ds(CHUNK * n + 16 * h, 16), :] = jnp.concatenate([top, rest], axis=1)

    def finish(group, side):
        sums = jnp.dot(squares[side], ones[...], preferred_element_type=jnp.float32)
        for n in range(GROUP):
            item = group * GROUP + n
            left = lefts[item]
            embeds = []
            for k in range(4):
                at = CHUNK * n + 8 * k
                total = sums[at : at + 8, :]
                embeds.append(raws[side, pl.ds(at, 8), :] * lax.rsqrt(total + 1e-06))
            first = jnp.broadcast_to(embeds[0][0:1, :], (8, DIM))
            embeds = [jnp.where(4 * sub + k < left, embeds[k], first) for k in range(4)]
            stored[items[item]] = jnp.concatenate(embeds, axis=0).astype(jnp.bfloat16)

    def body(i, carry):
        for side in range(2):
            group = 2 * i + side
            finish(jnp.maximum(group - 2, 0), side)
            decode(1 - side)
            gather(jnp.minimum(group, n_items // GROUP - 1), side)
        return carry

    def repeat(p, carry):
        for q in range(4):
            begin = 4 * (4 * p + q)
            last = lasts[4 * p + q]
            for c in range(1, 4):
                stored[begin + c] = stored[jnp.minimum(begin + c, last)]
        return carry

    n_pass = lasts.shape[0]

    def close(j):
        per = n_pass // parts
        lax.fori_loop(j * (per // 4), (j + 1) * (per // 4), repeat, 0)
        out_copy(j).start()

    def part(j, begin):
        codes_copy(j).wait()
        lax.fori_loop(begin, bounds[j], body, 0)

        @pl.when(j > 0)
        def _():
            close(j - 1)

        return bounds[j]

    lax.fori_loop(0, parts, part, jnp.int32(0))
    close(parts - 1)
    for j in range(parts):
        out_copy(j).wait()


def plan_items(lengths, parts):
    n_pass = lengths.shape[0]
    chunks = jnp.right_shift(lengths + (CHUNK - 1), 5)
    ends = jnp.cumsum(chunks)
    order = jnp.minimum(jnp.arange(4 * n_pass, dtype=jnp.int32), ends[-1] - 1)
    passed = ends[None, :] <= order[:, None]
    which = jnp.sum(passed.astype(jnp.int32), axis=1)
    begin = jnp.max(jnp.where(passed, ends[None, :], 0), axis=1)
    length = jnp.sum(jnp.where(jnp.arange(n_pass)[None, :] == which[:, None], lengths[None, :], 0), axis=1)
    ch = order - begin
    items = 4 * which + ch
    starts = (jnp.right_shift(which, 3) * CHUNK + ch * 8) * 8 + jnp.bitwise_and(which, 7)
    lefts = length - CHUNK * ch
    lasts = 4 * jnp.arange(n_pass, dtype=jnp.int32) + chunks - 1
    per = n_pass // parts
    bounds = jnp.right_shift(ends[per - 1 :: per], GROUP_BITS + 1)
    groups = jnp.right_shift(ends[-1] + (GROUP - 1), GROUP_BITS)
    bounds = jnp.where(jnp.arange(parts) == parts - 1, jnp.right_shift(groups + 3, 1), bounds)
    return items, starts, lefts, lasts, bounds


def unpack(ids, lengths, buckets, codes, centroids):
    n_pass = codes.shape[0]
    n_items = 4 * n_pass
    plan = plan_items(lengths, PARTS)
    tiles = codes.reshape(n_pass // 8, 8, CHUNK, DIM).transpose(0, 2, 1, 3).reshape(-1, DIM)
    by_place = ids.reshape(n_items, CHUNK).T.reshape(-1)
    smem = pl.BlockSpec(memory_space=pltpu.SMEM)
    anywhere = pl.BlockSpec(memory_space=pl.ANY)
    rows = GROUP * CHUNK
    return pl.pallas_call(
        unpack_kernel,
        in_specs=[smem] * 6 + [anywhere] * 3,
        out_specs=anywhere,
        out_shape=jax.ShapeDtypeStruct((n_items, CHUNK, DIM), jnp.bfloat16),
        scratch_shapes=[
            pltpu.VMEM(centroids.shape, jnp.float32),
            pltpu.VMEM((TAB_BUFS, TAB_STEP, DIM), jnp.bfloat16),
            pltpu.SMEM((n_pass * PTOK,), jnp.int32),
            pltpu.VMEM(tiles.shape, jnp.int32),
            pltpu.VMEM((n_items, CHUNK, DIM), jnp.bfloat16),
            pltpu.VMEM((2, rows, DIM), jnp.float32),
            pltpu.VMEM((2, 8 * GROUP, 4 * DIM), jnp.float32),
            pltpu.VMEM((2, rows, DIM), jnp.float32),
            pltpu.VMEM((2, rows, 2 * DIM), jnp.bfloat16),
            pltpu.VMEM((DIM, 4 * DIM), jnp.bfloat16),
            pltpu.VMEM((2 * DIM, DIM), jnp.bfloat16),
            pltpu.SemaphoreType.DMA((TAB_BUFS,)),
            pltpu.SemaphoreType.DMA,
            pltpu.SemaphoreType.DMA((PARTS,)),
            pltpu.SemaphoreType.DMA,
        ],
        compiler_params=pltpu.CompilerParams(vmem_limit_bytes=60 * 2**20),
        cost_estimate=pl.CostEstimate(flops=10**9, bytes_accessed=40 * 2**20, transcendentals=0),
        name="unpack",
    )(*plan, buckets, by_place, tiles, centroids)


def score_kernel(rows_per, slots, recv, stored_hbm, out, stored, best, sem):
    parts = sem.shape[0]
    size = stored.shape[0] // parts

    def copy(i):
        return pltpu.make_async_copy(
            stored_hbm.at[pl.ds(i * size, size)], stored.at[pl.ds(i * size, size)], sem.at[i]
        )

    for i in range(parts):
        copy(i).start()
    for i in range(parts):
        copy(i).wait()

    def one(src, which):
        q = recv[pl.ds(pl.multiple_of(src * rows_per + 32 * which, 16), 32), :]
        zero = jnp.zeros_like(q)
        pair_q = jnp.concatenate(
            [jnp.concatenate([q, zero], axis=1), jnp.concatenate([zero, q], axis=1)], axis=0
        )
        query = 2 * src + which
        sides = [[], []]
        for place in range(16):
            sides[place % 2].append(stored[slots[query * 16 + place]])
        both = jnp.concatenate([jnp.concatenate(side, axis=0) for side in sides], axis=1)
        sims = lax.dot_general(
            both, pair_q, (((1,), (1,)), ((), ())), preferred_element_type=jnp.float32
        )
        tops = [
            jnp.max(sims[PTOK * pair : PTOK * (pair + 1), :], axis=0, keepdims=True)
            for pair in range(8)
        ]
        best[pl.ds(query, 1), :] = jnp.concatenate(tops, axis=1)

    def body(src, carry):
        one(src, 0)
        one(src, 1)
        return carry

    lax.fori_loop(0, recv.shape[0] // rows_per, body, 0)
    width = best.shape[1]
    member = lax.broadcasted_iota(jnp.int32, (width, 16), 0) // 32
    member = member == lax.broadcasted_iota(jnp.int32, (width, 16), 1)
    out[...] = jnp.dot(
        best[...],
        member.astype(jnp.float32),
        precision=lax.Precision.HIGHEST,
        preferred_element_type=jnp.float32,
    )


def score(rows_per, slots, recv, stored):
    devices = recv.shape[0] // rows_per
    return pl.pallas_call(
        functools.partial(score_kernel, rows_per),
        in_specs=[
            pl.BlockSpec(memory_space=pltpu.SMEM),
            pl.BlockSpec(memory_space=pltpu.VMEM),
            pl.BlockSpec(memory_space=pl.ANY),
        ],
        out_specs=pl.BlockSpec(memory_space=pltpu.VMEM),
        out_shape=jax.ShapeDtypeStruct((2 * devices, 16), jnp.float32),
        scratch_shapes=[
            pltpu.VMEM((stored.size // (PTOK * DIM), PTOK, DIM), jnp.bfloat16),
            pltpu.VMEM((2 * devices, 16 * 32), jnp.float32),
            pltpu.SemaphoreType.DMA((16,)),
        ],
        compiler_params=pltpu.CompilerParams(vmem_limit_bytes=40 * 2**20),
        cost_estimate=pl.CostEstimate(flops=10**10, bytes_accessed=20 * 2**20, transcendentals=0),
        name="score",
    )(slots, recv, stored.reshape(-1, PTOK, DIM))


def local(queries, cand_dev, cand_slot, codes, cent_ids, lengths, centroids, buckets):
    devices = lax.axis_size(AXES)
    q_rows, k_top = cand_dev.shape
    per = cand_slot.shape[1] // k_top
    rows_per = 80
    hits = (cand_dev[:, :, None] == jnp.arange(devices, dtype=jnp.int32)).astype(jnp.int32)
    per_query = jnp.sum(hits, axis=1)
    before = jnp.cumsum(per_query, axis=0) - per_query
    place = jnp.sum(hits * before[:, None, :], axis=2)
    dest = (cand_dev * 2 + place).reshape(-1)
    route = jnp.arange(devices * 2, dtype=jnp.int32)[:, None] == dest[None, :]
    route_q = route.astype(jnp.bfloat16)
    spread = jnp.broadcast_to(
        queries[:, None], (q_rows, k_top) + queries.shape[1:]
    ).reshape(q_rows * k_top, -1)
    send_q = jnp.dot(route_q, spread, preferred_element_type=jnp.float32).astype(jnp.bfloat16)
    slot_rows = cand_slot.reshape(q_rows * k_top, per)
    halves = jnp.concatenate(
        [jnp.bitwise_and(slot_rows, 255), jnp.right_shift(slot_rows, 8)], axis=1
    ).astype(jnp.bfloat16)
    send_s = jnp.dot(route_q, halves, preferred_element_type=jnp.float32).astype(jnp.bfloat16)
    send = jnp.concatenate(
        [
            send_q.reshape(devices, 64, DIM),
            jnp.pad(send_s.reshape(devices, 1, 4 * per), ((0, 0), (0, rows_per - 65), (0, DIM - 4 * per))),
        ],
        axis=1,
    )
    recv = lax.all_to_all(send, AXES, split_axis=0, concat_axis=0, tiled=True)
    stored = unpack(cent_ids, lengths, buckets, codes, centroids)
    got = recv[:, 64, : 4 * per].astype(jnp.int32).reshape(devices * 2, 2 * per)
    slots = (got[:, :per] + 256 * got[:, per:]).reshape(-1)
    scored = score(rows_per, slots, recv.reshape(devices * rows_per, DIM), stored)
    returned = lax.all_to_all(
        scored.reshape(devices, 2, per), AXES, split_axis=0, concat_axis=0, tiled=True
    )
    result = jnp.dot(
        route.astype(jnp.float32).T,
        returned.reshape(devices * 2, per),
        precision=lax.Precision.HIGHEST,
        preferred_element_type=jnp.float32,
    )
    return result.reshape(q_rows, k_top * per)


def solution(mesh):
    in_specs = (
        P(AXES, None, None),
        P(AXES, None),
        P(AXES, None),
        P(AXES, None),
        P(AXES, None),
        P(AXES),
        P(),
        P(),
    )
    return jax.shard_map(
        local, mesh=mesh, in_specs=in_specs, out_specs=P(AXES, None), check_vma=False
    )
```

time: 1220 us -> 185 us (0.15)
  local copies, waits for them, and re-layouts: 981 us -> 9.81 us
  Pallas kernels: 0 us -> 129 us
  matrix products: 104 us -> 2.54 us
  other arithmetic: 75.2 us -> 9.82 us
  loops' own time: 15.3 us -> 0 us
    gather x35 -> x0, local copies, waits for them, and re-layouts: 674 us -> none  [the longest x16 388 us: block(): embed = jnp.take(stored, block_s, axis=0).reshape(step, per, PTOK, DIM)]
    while x16 -> x0, local copies, waits for them, and re-layouts: 147 us -> none
    pallas_call x0 -> x2, Pallas kernels: none -> 129 us  [the longest x1 71.5 us: score(): pl.pallas_call(functools.partial(score_kernel, rows_per), in_specs=[pl.Bl...]
    dot_general x19 -> x3, matrix products: 104 us -> 2.54 us  [the longest x1 2.08 us: local(): jnp.dot(route_q, spread, preferred_element_type=jnp.float32)]
    shift_right_arithmetic x8 -> x2, local copies, waits for them, and re-layouts: 101 us -> 0.18 us  [local(): jnp.right_shift(slot_rows, 8)]
    unnamed x12 -> x5, local copies, waits for them, and re-layouts: 53.7 us -> 0.78 us
    reduce_sum x17 -> x1, other arithmetic: 34.4 us -> 0.95 us  [plan_items(): jnp.sum(jnp.where(jnp.arange(n_pass)[None, :] == which[:, None], lengths[...]
    convert_element_type x2 -> x1, other arithmetic: 31.6 us -> 0.21 us  [local(): got = recv[:, 64, :4 * per].astype(jnp.int32).reshape(devices * 2, 2 * per)]
  transfers between devices with their start and end apart: 2 -> 1, of which waited for: 0 -> 0; matrix products, arithmetic and copies ran while one was open for 41% -> 5% of each run, Pallas kernels for 0% -> 31%
where the time goes in v1:
time: 185 us; the launch traced here: 184 us
  Pallas kernels  129 us (70%)
  blocking collectives  20.3 us (11%)
  starting transfers between devices  11.5 us (6%)
  other arithmetic  9.82 us (5%)
  local copies, waits for them, and re-layouts  9.81 us (5%)
  matrix products  2.54 us (1%)
    pallas_call x1, Pallas kernels, score(): pl.pallas_call(functools.partial(score_kernel, rows_per), in_specs=[pl.Bl...  71.5 us
    pallas_call x1, Pallas kernels, unpack(): pl.pallas_call(unpack_kernel, in_specs=[smem] * 6 + [anywhere] * 3, out_s...  57.2 us
    all_to_all x1, blocking collectives, local(): lax.all_to_all(scored.reshape(devices, 2, per), AXES, split_axis=0, conca...  20.3 us
    all_to_all x1, starting transfers between devices, local(): recv = lax.all_to_all(send, AXES, split_axis=0, concat_axis=0, tiled=True)  11.5 us
  transfers between devices with their start and end apart: 1, of which 0 were waited for; matrix products, arithmetic and copies ran while one was open for 5% of the time, Pallas kernels for 31%

profile of v1, /device:TPU:1, one launch (start us, length us, event | category | flops | bytes accessed | tf_op | source)
XLA Modules:
  0.0 184.1 jit_solution(4485069612391995512)
XLA Ops:
  0.0 0.8 convert_reduce_fusion
  0.8 1.0 select_reduce_fusion.1
  1.8 0.7 multiply_add_fusion.1
  2.6 0.7 and_convert_fusion
  3.4 0.1 shift_right_arithmetic.36
  3.6 0.2 convolution_convert_fusion.1
  3.8 0.1 copy.22
  3.9 0.1 reshape.120
  4.0 1.0 broadcast_in_dim.21
  5.0 2.1 %convolution_convert_fusion = bf16[256,4096]{1,0:T(8,128)(2,1)} fusion(bf16[16,8,32,128]{3,2,1,0:T(8,128)(2,1)S(1)} %bitcast.29, s32[128]{0:T(128)S(1)} %eq.48), kind=kOutput, calls=%fused_computation.4 | convolution fusion | flops 269516800 | bytes 3146240 | tf_op jit(solution)/shard_map/dot_general | solution.py:315
  7.1 2.9 %reshape.105 = bf16[128,64,128]{2,1,0:T(8,128)(2,1)S(1)} reshape(bf16[256,4096]{1,0:T(8,128)(2,1)} %convolution_convert_fusion) | data formatting | bytes 4194304 | tf_op jit(solution)/shard_map/reshape | solution.py:323
  10.0 1.8 fusion.3
  11.8 11.5 %all-to-all-start = ((bf16[128,80,128]{2,1,0:T(8,128)(2,1)}), bf16[128,80,128]{2,1,0:T(8,128)(2,1)S(1)}, u32[]{:S(2)}, u32[]{:S(2)}) async-start(bf16[128,80,128]{2,1,0:T(8,128)(2,1)} %fusion.3), calls=%async_computation | async-start | bytes 5242880 | tf_op jit(solution)/shard_map/all_to_all | solution.py:328
  23.4 0.6 add_add_fusion
  24.0 0.3 reduce-window.9
  24.4 0.1 slice_reduce_fusion
  24.6 0.6 slice.28
  26.6 1.3 reshape.111
  27.8 1.5 copy.24
  29.3 0.8 copy.29
  30.1 1.4 fusion.2
  31.5 1.0 select_reduce_fusion
  32.5 0.6 compare_select_fusion.1.bounds
  33.0 0.6 and_add_fusion
  33.6 57.2 %unpack.1 = bf16[2048,32,128]{2,1,0:T(8,128)(2,1)} custom-call(s32[2048]{0:T(1024)} %get-tuple-element.8.items, s32[2048]{0:T(1024)} %get-tuple-element.7.starts, s32[2048]{0:T(1024)} %get-tuple-element.9.lefts, s32[512]{0:T(512)} %get-tuple-element.12.lasts, s32[8]{0:T(128)} %compare_select_fusion.1.bounds, f32[4]{0:T(128)} %buckets.1, s32[65536]{0:T(1024)} %bitcast.30, ...), custom_call_target="tpu_custom_call" | custom-call | flops 1000000000 | bytes 41943040 | tf_op jit(solution)/shard_map/unpack/pallas_call | solution.py:199
  90.8 0.2 fusion.8
  91.1 0.1 fusion.6
  91.2 0.1 reshape.107.slots
  91.3 71.5 %score.1 = f32[256,16]{1,0:T(8,128)S(1)} custom-call(s32[4096]{0:T(1024)S(1)} %reshape.107.slots, bf16[10240,128]{1,0:T(8,128)(2,1)S(1)} %bitcast.24, bf16[512,128,128]{2,1,0:T(8,128)(2,1)} %bitcast.26), custom_call_target="tpu_custom_call" | custom-call | flops 10000000000 | bytes 20971520 | tf_op jit(solution)/shard_map/score/pallas_call | solution.py:280
  162.8 20.3 %all_to_all.10 = f32[128,2,16]{2,1,0:T(2,128)S(1)} all-to-all(f32[128,2,16]{2,1,0:T(2,128)S(1)} %bitcast.25), channel_id=1, replica_groups=mesh['corpus'=32,'replica'=4] {'corpus','replica'}, dimensions={0} | all-to-all | bytes 32768 | tf_op jit(solution)/shard_map/all_to_all | solution.py:333
  183.1 0.3 fusion.7
  183.4 0.7 reshape.118
  (17 shorter events, 0.7 us)
Async XLA Ops:
  10.0 13.4 %copy-start.1 = (s32[512]{0:T(512)S(1)}, s32[512]{0:T(512)}, u32[]{:S(2)}) copy-start(s32[512]{0:T(512)} %param.13) | copy-start | bytes 6148
  10.0 16.5 %copy-start = (s32[512,128]{1,0:T(8,128)S(1)}, s32[512,128]{1,0:T(8,128)}, u32[]{:S(2)}) copy-start(s32[512,128]{1,0:T(8,128)} %param.12) | copy-start | bytes 786436
  11.8 79.0 %all-to-all-start = ((bf16[128,80,128]{2,1,0:T(8,128)(2,1)}), bf16[128,80,128]{2,1,0:T(8,128)(2,1)S(1)}, u32[]{:S(2)}, u32[]{:S(2)}) async-start(bf16[128,80,128]{2,1,0:T(8,128)(2,1)} %fusion.3), calls=%async_computation | async-start | bytes 5242880 | tf_op jit(solution)/shard_map/all_to_all | solution.py:328

commit v2 on v1

--- a/solution.py
+++ b/solution.py
@@ -15,6 +15,9 @@
 TAB_STEP = 1024
 TAB_BUFS = 10
 GROUP_BITS = 3
+TURN_BITS = 1
+TURN = 1 << TURN_BITS
+SCORE_TURN = 8
 GROUP = 1 << GROUP_BITS
 PARTS = 8
 
@@ -128,9 +131,10 @@
             stored[items[item]] = jnp.concatenate(embeds, axis=0).astype(jnp.bfloat16)
 
     def body(i, carry):
-        for side in range(2):
-            group = 2 * i + side
-            finish(jnp.maximum(group - 2, 0), side)
+        for turn in range(TURN):
+            group = TURN * i + turn
+            side = turn % 2
+            finish(jnp.clip(group - 2, 0, n_items // GROUP - 1), side)
             decode(1 - side)
             gather(jnp.minimum(group, n_items // GROUP - 1), side)
         return carry
@@ -181,9 +185,9 @@
     lefts = length - CHUNK * ch
     lasts = 4 * jnp.arange(n_pass, dtype=jnp.int32) + chunks - 1
     per = n_pass // parts
-    bounds = jnp.right_shift(ends[per - 1 :: per], GROUP_BITS + 1)
+    bounds = jnp.right_shift(ends[per - 1 :: per], GROUP_BITS + TURN_BITS)
     groups = jnp.right_shift(ends[-1] + (GROUP - 1), GROUP_BITS)
-    bounds = jnp.where(jnp.arange(parts) == parts - 1, jnp.right_shift(groups + 3, 1), bounds)
+    bounds = jnp.where(jnp.arange(parts) == parts - 1, jnp.right_shift(groups + TURN + 1, TURN_BITS), bounds)
     return items, starts, lefts, lasts, bounds
 
 
@@ -259,11 +263,12 @@
         best[pl.ds(query, 1), :] = jnp.concatenate(tops, axis=1)
 
     def body(src, carry):
-        one(src, 0)
-        one(src, 1)
+        for j in range(SCORE_TURN):
+            one(SCORE_TURN * src + j, 0)
+            one(SCORE_TURN * src + j, 1)
         return carry
 
-    lax.fori_loop(0, recv.shape[0] // rows_per, body, 0)
+    lax.fori_loop(0, recv.shape[0] // rows_per // SCORE_TURN, body, 0)
     width = best.shape[1]
     member = lax.broadcasted_iota(jnp.int32, (width, 16), 0) // 32
     member = member == lax.broadcasted_iota(jnp.int32, (width, 16), 1)

time: 185 us -> 159 us (0.86)
  Pallas kernels: 129 us -> 102 us
    pallas_call x1, Pallas kernels: 71.5 us -> 46.1 us  [score(): pl.pallas_call(functools.partial(score_kernel, rows_per), in_specs=[pl.Bl...]
  transfers between devices with their start and end apart: 1 -> 1, of which waited for: 0 -> 0; matrix products, arithmetic and copies ran while one was open for 5% -> 6% of each run, Pallas kernels for 31% -> 36%
where the time goes in v2:
time: 159 us; the launch traced here: 158 us
  Pallas kernels  102 us (64%)
  blocking collectives  20.7 us (13%)
  starting transfers between devices  11.5 us (7%)
  other arithmetic  9.82 us (6%)
  local copies, waits for them, and re-layouts  9.81 us (6%)
  matrix products  2.54 us (2%)
    pallas_call x1, Pallas kernels, unpack(): pl.pallas_call(unpack_kernel, in_specs=[smem] * 6 + [anywhere] * 3, out_s...  56.3 us
    pallas_call x1, Pallas kernels, score(): pl.pallas_call(functools.partial(score_kernel, rows_per), in_specs=[pl.Bl...  46.1 us
    all_to_all x1, blocking collectives, local(): lax.all_to_all(scored.reshape(devices, 2, per), AXES, split_axis=0, conca...  20.7 us
    all_to_all x1, starting transfers between devices, local(): recv = lax.all_to_all(send, AXES, split_axis=0, concat_axis=0, tiled=True)  11.5 us
  transfers between devices with their start and end apart: 1, of which 0 were waited for; matrix products, arithmetic and copies ran while one was open for 6% of the time, Pallas kernels for 36%

profile of v2, /device:TPU:1, one launch (start us, length us, event | category | flops | bytes accessed | tf_op | source)
XLA Modules:
  0.0 158.3 jit_solution(739371493360499369)
XLA Ops:
  0.0 0.8 convert_reduce_fusion
  0.8 1.0 select_reduce_fusion.1
  1.8 0.7 multiply_add_fusion.1
  2.6 0.7 and_convert_fusion
  3.4 0.1 shift_right_arithmetic.36
  3.6 0.2 convolution_convert_fusion.1
  3.8 0.1 copy.22
  3.9 0.1 reshape.120
  4.0 1.0 broadcast_in_dim.21
  5.0 2.1 %convolution_convert_fusion = bf16[256,4096]{1,0:T(8,128)(2,1)} fusion(bf16[16,8,32,128]{3,2,1,0:T(8,128)(2,1)S(1)} %bitcast.29, s32[128]{0:T(128)S(1)} %eq.48), kind=kOutput, calls=%fused_computation.4 | convolution fusion | flops 269516800 | bytes 3146240 | tf_op jit(solution)/shard_map/dot_general | solution.py:320
  7.1 2.9 %reshape.105 = bf16[128,64,128]{2,1,0:T(8,128)(2,1)S(1)} reshape(bf16[256,4096]{1,0:T(8,128)(2,1)} %convolution_convert_fusion) | data formatting | bytes 4194304 | tf_op jit(solution)/shard_map/reshape | solution.py:328
  10.0 1.8 %fusion.3 = bf16[128,80,128]{2,1,0:T(8,128)(2,1)} fusion(bf16[128,1,64]{2,1,0:T(2,128)(2,1)S(1)} %reshape.120, bf16[128,64,128]{2,1,0:T(8,128)(2,1)S(1)} %reshape.105), kind=kLoop, calls=%fused_computation.9 | loop fusion | flops 7864320 | bytes 4734976 | tf_op jit(solution)/shard_map/concatenate | solution.py:326
  11.8 11.5 %all-to-all-start = ((bf16[128,80,128]{2,1,0:T(8,128)(2,1)}), bf16[128,80,128]{2,1,0:T(8,128)(2,1)S(1)}, u32[]{:S(2)}, u32[]{:S(2)}) async-start(bf16[128,80,128]{2,1,0:T(8,128)(2,1)} %fusion.3), calls=%async_computation | async-start | bytes 5242880 | tf_op jit(solution)/shard_map/all_to_all | solution.py:333
  23.4 0.6 add_add_fusion
  24.0 0.3 reduce-window.9
  24.4 0.1 slice_reduce_fusion
  24.6 0.6 slice.28
  26.6 1.3 reshape.111
  27.8 1.5 copy.24
  29.3 0.8 copy.29
  30.1 1.4 fusion.2
  31.5 1.0 select_reduce_fusion
  32.5 0.6 compare_select_fusion.1.bounds
  33.0 0.6 and_add_fusion
  33.6 56.3 %unpack.1 = bf16[2048,32,128]{2,1,0:T(8,128)(2,1)} custom-call(s32[2048]{0:T(1024)} %get-tuple-element.8.items, s32[2048]{0:T(1024)} %get-tuple-element.7.starts, s32[2048]{0:T(1024)} %get-tuple-element.9.lefts, s32[512]{0:T(512)} %get-tuple-element.12.lasts, s32[8]{0:T(128)} %compare_select_fusion.1.bounds, f32[4]{0:T(128)} %buckets.1, s32[65536]{0:T(1024)} %bitcast.30, ...), custom_call_target="tpu_custom_call" | custom-call | flops 1000000000 | bytes 41943040 | tf_op jit(solution)/shard_map/unpack/pallas_call | solution.py:203
  89.9 0.2 fusion.8
  90.2 0.1 fusion.6
  90.3 0.1 reshape.107.slots
  90.5 46.1 %score.1 = f32[256,16]{1,0:T(8,128)S(1)} custom-call(s32[4096]{0:T(1024)S(1)} %reshape.107.slots, bf16[10240,128]{1,0:T(8,128)(2,1)S(1)} %bitcast.24, bf16[512,128,128]{2,1,0:T(8,128)(2,1)} %bitcast.26), custom_call_target="tpu_custom_call" | custom-call | flops 10000000000 | bytes 20971520 | tf_op jit(solution)/shard_map/score/pallas_call | solution.py:285
  136.6 20.7 %all_to_all.10 = f32[128,2,16]{2,1,0:T(2,128)S(1)} all-to-all(f32[128,2,16]{2,1,0:T(2,128)S(1)} %bitcast.25), channel_id=1, replica_groups=mesh['corpus'=32,'replica'=4] {'corpus','replica'}, dimensions={0} | all-to-all | bytes 32768 | tf_op jit(solution)/shard_map/all_to_all | solution.py:338
  157.3 0.3 fusion.7
  157.6 0.7 reshape.118
  (17 shorter events, 0.7 us)
Async XLA Ops:
  10.0 13.4 %copy-start.1 = (s32[512]{0:T(512)S(1)}, s32[512]{0:T(512)}, u32[]{:S(2)}) copy-start(s32[512]{0:T(512)} %param.13) | copy-start | bytes 6148
  10.0 16.5 %copy-start = (s32[512,128]{1,0:T(8,128)S(1)}, s32[512,128]{1,0:T(8,128)}, u32[]{:S(2)}) copy-start(s32[512,128]{1,0:T(8,128)} %param.12) | copy-start | bytes 786436
  11.8 78.1 %all-to-all-start = ((bf16[128,80,128]{2,1,0:T(8,128)(2,1)}), bf16[128,80,128]{2,1,0:T(8,128)(2,1)S(1)}, u32[]{:S(2)}, u32[]{:S(2)}) async-start(bf16[128,80,128]{2,1,0:T(8,128)(2,1)} %fusion.3), calls=%async_computation | async-start | bytes 5242880 | tf_op jit(solution)/shard_map/all_to_all | solution.py:333

commit v3 on v2

--- a/solution.py
+++ b/solution.py
@@ -20,9 +20,11 @@
 SCORE_TURN = 8
 GROUP = 1 << GROUP_BITS
 PARTS = 8
-
-
-def load_table(cent, tab, buf, sem):
+SPARE = 48
+SEND_ROWS = 96
+
+
+def load_table(cent, tab, buf, sem, beside):
     steps = cent.shape[0] // TAB_STEP
 
     def copy(i, slot):
@@ -41,17 +43,19 @@
         copy(i, slot).wait()
         start = pl.multiple_of(i * TAB_STEP, TAB_STEP)
         tab[pl.ds(start, TAB_STEP), :] = buf[slot].astype(jnp.float32)
-        return carry
-
-    lax.fori_loop(0, steps, body, 0)
+        return beside(i, carry)
+
+    return lax.fori_loop(0, steps, body, jnp.int32(0))
 
 
 def unpack_kernel(
-    items, starts, lefts, lasts, bounds, buckets, ids_hbm, codes_hbm, cent, out,
+    lens, buckets, ids_hbm, codes_hbm, cent, out,
+    items, keys, starts, lefts, bounds,
     tab, buf, ids, codes, stored, centre, words, raws, squares, spread_of, ones,
     sem, ids_sem, codes_sem, out_sem,
 ):
-    n_items = items.shape[0]
+    n_pass = lens.shape[0]
+    n_items = 4 * n_pass
     parts = codes_sem.shape[0]
     code_rows = codes.shape[0] // parts
     part_chunks = n_items // parts
@@ -79,21 +83,45 @@
     words[1] = jnp.zeros_like(words[1])
     raws[...] = jnp.zeros_like(raws)
     squares[...] = jnp.zeros_like(squares)
-    load_table(cent, tab, buf, sem)
+    table_steps = cent.shape[0] // TAB_STEP
+    per_step = n_pass // table_steps
+
+    def plan(i, count):
+        for q in range(per_step):
+            p = i * per_step + q
+            length = lens[p]
+            first = jnp.left_shift(jnp.right_shift(p, 3), 8) + jnp.bitwise_and(p, 7)
+            for c in range(4):
+                items[count + c] = 4 * p + c
+                keys[count + c] = p + c * CHUNK * n_pass
+                starts[count + c] = first + 64 * c
+                lefts[count + c] = length - CHUNK * c
+            count = count + jnp.right_shift(length + (CHUNK - 1), 5)
+        bounds[i // (table_steps // parts)] = jnp.right_shift(count, GROUP_BITS + TURN_BITS)
+        return count
+
+    count = load_table(cent, tab, buf, sem, plan)
+    for extra in range(SPARE):
+        for ref in (items, keys, starts, lefts):
+            ref[count + extra] = ref[count - 1]
+    groups = jnp.right_shift(count + (GROUP - 1), GROUP_BITS)
+    bounds[parts - 1] = jnp.right_shift(groups + TURN + 1, TURN_BITS)
     for j in range(1, parts):
         codes_copy(j).start()
     ids_copy.wait()
     b0, b1, b2, b3 = (buckets[i] for i in range(4))
 
+    reach = n_pass * (PTOK - CHUNK + 1)
+
     def gather(group, side):
         code_rows = []
         for n in range(GROUP):
             item = group * GROUP + n
-            code = items[item]
+            key = keys[item]
             code_rows.append(codes[pl.ds(starts[item], 8, stride=8), :])
             for k in range(4):
                 for r in range(8):
-                    token = ids.at[pl.ds((4 * r + k) * n_items, n_items)][code]
+                    token = ids.at[pl.ds((4 * r + k) * n_pass, reach)][key]
                     centre[side, pl.ds(CHUNK * n + 8 * k + r, 1), :] = tab[pl.ds(token, 1), :]
         packed = jnp.concatenate(code_rows, axis=0).astype(jnp.float32).astype(jnp.bfloat16)
         words[side] = jnp.dot(packed, spread_of[...], preferred_element_type=jnp.float32)
@@ -142,12 +170,10 @@
     def repeat(p, carry):
         for q in range(4):
             begin = 4 * (4 * p + q)
-            last = lasts[4 * p + q]
+            last = begin + jnp.right_shift(lens[4 * p + q] + (CHUNK - 1), 5) - 1
             for c in range(1, 4):
                 stored[begin + c] = stored[jnp.minimum(begin + c, last)]
         return carry
-
-    n_pass = lasts.shape[0]
 
     def close(j):
         per = n_pass // parts
@@ -170,42 +196,22 @@
         out_copy(j).wait()
 
 
-def plan_items(lengths, parts):
-    n_pass = lengths.shape[0]
-    chunks = jnp.right_shift(lengths + (CHUNK - 1), 5)
-    ends = jnp.cumsum(chunks)
-    order = jnp.minimum(jnp.arange(4 * n_pass, dtype=jnp.int32), ends[-1] - 1)
-    passed = ends[None, :] <= order[:, None]
-    which = jnp.sum(passed.astype(jnp.int32), axis=1)
-    begin = jnp.max(jnp.where(passed, ends[None, :], 0), axis=1)
-    length = jnp.sum(jnp.where(jnp.arange(n_pass)[None, :] == which[:, None], lengths[None, :], 0), axis=1)
-    ch = order - begin
-    items = 4 * which + ch
-    starts = (jnp.right_shift(which, 3) * CHUNK + ch * 8) * 8 + jnp.bitwise_and(which, 7)
-    lefts = length - CHUNK * ch
-    lasts = 4 * jnp.arange(n_pass, dtype=jnp.int32) + chunks - 1
-    per = n_pass // parts
-    bounds = jnp.right_shift(ends[per - 1 :: per], GROUP_BITS + TURN_BITS)
-    groups = jnp.right_shift(ends[-1] + (GROUP - 1), GROUP_BITS)
-    bounds = jnp.where(jnp.arange(parts) == parts - 1, jnp.right_shift(groups + TURN + 1, TURN_BITS), bounds)
-    return items, starts, lefts, lasts, bounds
-
-
 def unpack(ids, lengths, buckets, codes, centroids):
     n_pass = codes.shape[0]
     n_items = 4 * n_pass
-    plan = plan_items(lengths, PARTS)
     tiles = codes.reshape(n_pass // 8, 8, CHUNK, DIM).transpose(0, 2, 1, 3).reshape(-1, DIM)
-    by_place = ids.reshape(n_items, CHUNK).T.reshape(-1)
+    by_place = ids.T.reshape(-1)
     smem = pl.BlockSpec(memory_space=pltpu.SMEM)
     anywhere = pl.BlockSpec(memory_space=pl.ANY)
     rows = GROUP * CHUNK
     return pl.pallas_call(
         unpack_kernel,
-        in_specs=[smem] * 6 + [anywhere] * 3,
+        in_specs=[smem] * 2 + [anywhere] * 3,
         out_specs=anywhere,
         out_shape=jax.ShapeDtypeStruct((n_items, CHUNK, DIM), jnp.bfloat16),
-        scratch_shapes=[
+        scratch_shapes=[pltpu.SMEM((n_items + SPARE,), jnp.int32)] * 4
+        + [
+            pltpu.SMEM((PARTS,), jnp.int32),
             pltpu.VMEM(centroids.shape, jnp.float32),
             pltpu.VMEM((TAB_BUFS, TAB_STEP, DIM), jnp.bfloat16),
             pltpu.SMEM((n_pass * PTOK,), jnp.int32),
@@ -225,7 +231,7 @@
         compiler_params=pltpu.CompilerParams(vmem_limit_bytes=60 * 2**20),
         cost_estimate=pl.CostEstimate(flops=10**9, bytes_accessed=40 * 2**20, transcendentals=0),
         name="unpack",
-    )(*plan, buckets, by_place, tiles, centroids)
+    )(lengths, buckets, by_place, tiles, centroids)
 
 
 def score_kernel(rows_per, slots, recv, stored_hbm, out, stored, best, sem):
@@ -302,44 +308,71 @@
     )(slots, recv, stored.reshape(-1, PTOK, DIM))
 
 
+def address_kernel(cand, queries, slots, send, dest, seen):
+    devices = seen.shape[0]
+    q_rows, k_top = cand.shape
+    per = slots.shape[1] // k_top
+    send[...] = jnp.zeros_like(send)
+    for d in range(devices):
+        seen[d] = 0
+    listed = slots[...]
+    low = jnp.bitwise_and(listed, 255).astype(jnp.float32)
+    high = jnp.right_shift(listed, 8).astype(jnp.float32)
+    in_row = DIM // per
+    for t in range(k_top):
+        row = t // in_row
+        turn = (in_row - t % in_row) * per % DIM
+        pieces = [
+            pltpu.roll(part[:, row * DIM : (row + 1) * DIM], turn, 1) if turn else part[:, row * DIM : (row + 1) * DIM]
+            for part in (low, high)
+        ]
+        for q in range(q_rows):
+            device = cand[q, t]
+            place = seen[device]
+            seen[device] = 1
+            dest[q * k_top + t] = 2 * device + place
+            base = pl.multiple_of(device * SEND_ROWS + 32 * place, 16)
+            send[pl.ds(base, 32), :] = queries[q]
+            meta = [jnp.broadcast_to(piece[q : q + 1, :], (8, DIM)) for piece in pieces]
+            at = pl.multiple_of(device * SEND_ROWS + 64 + 16 * place, 16)
+            send[pl.ds(at, 16), :] = jnp.concatenate(meta, axis=0).astype(jnp.bfloat16)
+
+
+def address(cand_dev, queries, cand_slot, devices):
+    smem = pl.BlockSpec(memory_space=pltpu.SMEM)
+    vmem = pl.BlockSpec(memory_space=pltpu.VMEM)
+    return pl.pallas_call(
+        address_kernel,
+        in_specs=[smem, vmem, vmem],
+        out_specs=[vmem, smem],
+        out_shape=[
+            jax.ShapeDtypeStruct((devices * SEND_ROWS, DIM), jnp.bfloat16),
+            jax.ShapeDtypeStruct((cand_dev.size,), jnp.int32),
+        ],
+        scratch_shapes=[pltpu.SMEM((devices,), jnp.int32)],
+        compiler_params=pltpu.CompilerParams(vmem_limit_bytes=24 * 2**20),
+        name="address",
+    )(cand_dev, queries, cand_slot)
+
+
 def local(queries, cand_dev, cand_slot, codes, cent_ids, lengths, centroids, buckets):
     devices = lax.axis_size(AXES)
     q_rows, k_top = cand_dev.shape
     per = cand_slot.shape[1] // k_top
-    rows_per = 80
-    hits = (cand_dev[:, :, None] == jnp.arange(devices, dtype=jnp.int32)).astype(jnp.int32)
-    per_query = jnp.sum(hits, axis=1)
-    before = jnp.cumsum(per_query, axis=0) - per_query
-    place = jnp.sum(hits * before[:, None, :], axis=2)
-    dest = (cand_dev * 2 + place).reshape(-1)
-    route = jnp.arange(devices * 2, dtype=jnp.int32)[:, None] == dest[None, :]
-    route_q = route.astype(jnp.bfloat16)
-    spread = jnp.broadcast_to(
-        queries[:, None], (q_rows, k_top) + queries.shape[1:]
-    ).reshape(q_rows * k_top, -1)
-    send_q = jnp.dot(route_q, spread, preferred_element_type=jnp.float32).astype(jnp.bfloat16)
-    slot_rows = cand_slot.reshape(q_rows * k_top, per)
-    halves = jnp.concatenate(
-        [jnp.bitwise_and(slot_rows, 255), jnp.right_shift(slot_rows, 8)], axis=1
-    ).astype(jnp.bfloat16)
-    send_s = jnp.dot(route_q, halves, preferred_element_type=jnp.float32).astype(jnp.bfloat16)
-    send = jnp.concatenate(
-        [
-            send_q.reshape(devices, 64, DIM),
-            jnp.pad(send_s.reshape(devices, 1, 4 * per), ((0, 0), (0, rows_per - 65), (0, DIM - 4 * per))),
-        ],
-        axis=1,
-    )
-    recv = lax.all_to_all(send, AXES, split_axis=0, concat_axis=0, tiled=True)
+    send, dest = address(cand_dev, queries, cand_slot, devices)
+    recv = lax.all_to_all(
+        send.reshape(devices, SEND_ROWS, DIM), AXES, split_axis=0, concat_axis=0, tiled=True
+    )
     stored = unpack(cent_ids, lengths, buckets, codes, centroids)
-    got = recv[:, 64, : 4 * per].astype(jnp.int32).reshape(devices * 2, 2 * per)
-    slots = (got[:, :per] + 256 * got[:, per:]).reshape(-1)
-    scored = score(rows_per, slots, recv.reshape(devices * rows_per, DIM), stored)
+    got = recv.reshape(devices, SEND_ROWS // 8, 8, DIM)[:, 8:, 0, :per].astype(jnp.int32)
+    slots = (got[:, 0::2] + 256 * got[:, 1::2]).reshape(-1)
+    scored = score(SEND_ROWS, slots, recv.reshape(devices * SEND_ROWS, DIM), stored)
     returned = lax.all_to_all(
         scored.reshape(devices, 2, per), AXES, split_axis=0, concat_axis=0, tiled=True
     )
+    route = jnp.arange(devices * 2, dtype=jnp.int32)[None, :] == dest[:, None]
     result = jnp.dot(
-        route.astype(jnp.float32).T,
+        route.astype(jnp.float32),
         returned.reshape(devices * 2, per),
         precision=lax.Precision.HIGHEST,
         preferred_element_type=jnp.float32,

time: 159 us -> 151 us (0.950)
  other arithmetic: 9.82 us -> 1.23 us
  Pallas kernels: 102 us -> 108 us
  matrix products: 2.54 us -> 0.25 us
    pallas_call x1 -> x2, Pallas kernels: 56.3 us -> 61.8 us  [the longest x1 59.5 us: unpack(): pl.pallas_call(unpack_kernel, in_specs=[smem] * 2 + [anywhere] * 3, out_s...]
    reshape x4 -> x1, local copies, waits for them, and re-layouts: 4.33 us -> 0.18 us  [local(): slots = (got[:, 0::2] + 256 * got[:, 1::2]).reshape(-1)]
    unnamed x5 -> x9, local copies, waits for them, and re-layouts: 0.78 us -> 4.63 us
    reduce_sum x3 -> x0, other arithmetic: 2.7 us -> none  [the longest x1 0.97 us: local(): place = jnp.sum(hits * before[:, None, :], axis=2)]
    dot_general x3 -> x1, matrix products: 2.54 us -> 0.25 us  [local(): jnp.dot(route.astype(jnp.float32), returned.reshape(devices * 2, per), pr...]
    slice x3 -> x2, local copies, waits for them, and re-layouts: 0.76 us -> 2.83 us  [local(): slots = (got[:, 0::2] + 256 * got[:, 1::2]).reshape(-1)]
    concatenate x1 -> x0, other arithmetic: 1.83 us -> none  [local(): jnp.concatenate([send_q.reshape(devices, 64, DIM), jnp.pad(send_s.reshape...]
  transfers between devices with their start and end apart: 1 -> 1, of which waited for: 0 -> 0; matrix products, arithmetic and copies ran while one was open for 6% -> 1% of each run, Pallas kernels for 36% -> 39%
where the time goes in v3:
time: 151 us
  Pallas kernels  108 us (72%)
  blocking collectives  20.4 us (14%)
  starting transfers between devices  11.5 us (8%)
  local copies, waits for them, and re-layouts  9.41 us (6%)
    pallas_call x1, Pallas kernels, unpack(): pl.pallas_call(unpack_kernel, in_specs=[smem] * 2 + [anywhere] * 3, out_s...  59.5 us
    pallas_call x1, Pallas kernels, score(): pl.pallas_call(functools.partial(score_kernel, rows_per), in_specs=[pl.Bl...  46.1 us
    all_to_all x1, blocking collectives, local(): lax.all_to_all(scored.reshape(devices, 2, per), AXES, split_axis=0, conca...  20.4 us
    all_to_all x1, starting transfers between devices, local(): lax.all_to_all(send.reshape(devices, SEND_ROWS, DIM), AXES, split_axis=0,...  11.5 us
    unnamed x9, local copies, waits for them, and re-layouts  4.63 us
  transfers between devices with their start and end apart: 1, of which 0 were waited for; matrix products, arithmetic and copies ran while one was open for 1% of the time, Pallas kernels for 39%

profile of v3, /device:TPU:1, one launch (start us, length us, event | category | flops | bytes accessed | tf_op | source)
XLA Modules:
  0.0 150.7 jit_solution(15324471919939750937)
XLA Ops:
  0.0 0.0 copy-start.1
  0.0 0.8 copy-done.1
  0.8 0.0 copy-start.2
  0.8 0.7 copy-done.2
  1.5 0.0 copy-start.3
  1.5 0.7 copy-done.3
  2.2 2.2 %address.1 = (bf16[12288,128]{1,0:T(8,128)(2,1)S(1)}, s32[128]{0:T(128)S(1)}) custom-call(s32[8,16]{1,0:T(8,128)S(1)} %copy-done.3, bf16[8,32,128]{2,1,0:T(8,128)(2,1)S(1)} %copy-done.1, s32[8,256]{1,0:T(8,128)S(1)} %copy-done.2), custom_call_target="tpu_custom_call" | custom-call | tf_op jit(solution)/shard_map/address/pallas_call | solution.py:344
  4.5 0.0 copy-start
  4.5 1.6 %copy-done = bf16[12288,128]{1,0:T(8,128)(2,1)} copy-done((bf16[12288,128]{1,0:T(8,128)(2,1)}, bf16[12288,128]{1,0:T(8,128)(2,1)S(1)}, u32[]{:S(2)}) %copy-start) | copy-done | bytes 3145752
  6.1 11.5 %all-to-all-start = ((bf16[128,96,128]{2,1,0:T(8,128)(2,1)}), bf16[128,96,128]{2,1,0:T(8,128)(2,1)S(1)}, u32[]{:S(2)}, u32[]{:S(2)}) async-start(bf16[128,96,128]{2,1,0:T(8,128)(2,1)} %bitcast.18), calls=%async_computation | async-start | bytes 6291456 | tf_op jit(solution)/shard_map/all_to_all | solution.py:363
  17.6 1.1 copy.11
  18.7 0.8 copy.14
  19.5 59.5 %unpack.1 = bf16[2048,32,128]{2,1,0:T(8,128)(2,1)} custom-call(s32[512]{0:T(512)} %lens.1, f32[4]{0:T(128)} %buckets.1, s32[65536]{0:T(1024)} %bitcast.22, s32[16384,128]{1,0:T(8,128)} %bitcast.21, bf16[65536,128]{1,0:T(8,128)(2,1)} %cent.1), custom_call_target="tpu_custom_call" | custom-call | flops 1000000000 | bytes 41943040 | tf_op jit(solution)/shard_map/unpack/pallas_call | solution.py:207
  79.0 0.0 all-to-all-done
  79.0 0.2 slice_convert_fusion
  79.2 0.8 slice.11
  80.0 2.1 %slice.10 = s32[128,2,16]{2,1,0:T(2,128)} slice(s32[128,4,16]{2,1,0:T(4,128)S(1)} %bitcast.24), slice={[0:128:1], [0:4:2], [0:16:1]} | slice | bytes 32768 | tf_op jit(solution)/shard_map/slice | solution.py:368
  82.1 1.0 multiply_add_fusion
  83.1 0.2 reshape.38.slots
  83.3 46.1 %score.1 = f32[256,16]{1,0:T(8,128)S(1)} custom-call(s32[4096]{0:T(1024)S(1)} %reshape.38.slots, bf16[12288,128]{1,0:T(8,128)(2,1)S(1)} %bitcast.17, bf16[512,128,128]{2,1,0:T(8,128)(2,1)} %bitcast.20), custom_call_target="tpu_custom_call" | custom-call | flops 10000000000 | bytes 20971520 | tf_op jit(solution)/shard_map/score/pallas_call | solution.py:291
  129.4 20.4 %all_to_all.10 = f32[128,2,16]{2,1,0:T(2,128)S(1)} all-to-all(f32[128,2,16]{2,1,0:T(2,128)S(1)} %bitcast.19), channel_id=1, replica_groups=mesh['corpus'=32,'replica'=4] {'corpus','replica'}, dimensions={0} | all-to-all | bytes 32768 | tf_op jit(solution)/shard_map/all_to_all | solution.py:370
  149.7 0.3 fusion
  150.0 0.7 reshape.46
Async XLA Ops:
  0.0 0.8 copy-start.1
  0.8 0.7 copy-start.2
  1.5 0.7 copy-start.3
  4.5 1.6 %copy-start = (bf16[12288,128]{1,0:T(8,128)(2,1)}, bf16[12288,128]{1,0:T(8,128)(2,1)S(1)}, u32[]{:S(2)}) copy-start(bf16[12288,128]{1,0:T(8,128)(2,1)S(1)} %get-tuple-element.8) | copy-start | bytes 9437188
  6.1 72.9 %all-to-all-start = ((bf16[128,96,128]{2,1,0:T(8,128)(2,1)}), bf16[128,96,128]{2,1,0:T(8,128)(2,1)S(1)}, u32[]{:S(2)}, u32[]{:S(2)}) async-start(bf16[128,96,128]{2,1,0:T(8,128)(2,1)} %bitcast.18), calls=%async_computation | async-start | bytes 6291456 | tf_op jit(solution)/shard_map/all_to_all | solution.py:363

commit v4 on v3

--- a/solution.py
+++ b/solution.py
@@ -17,7 +17,7 @@
 GROUP_BITS = 3
 TURN_BITS = 1
 TURN = 1 << TURN_BITS
-SCORE_TURN = 8
+SCORE_TURN = 16
 GROUP = 1 << GROUP_BITS
 PARTS = 8
 SPARE = 48
@@ -92,10 +92,13 @@
             length = lens[p]
             first = jnp.left_shift(jnp.right_shift(p, 3), 8) + jnp.bitwise_and(p, 7)
             for c in range(4):
-                items[count + c] = 4 * p + c
-                keys[count + c] = p + c * CHUNK * n_pass
-                starts[count + c] = first + 64 * c
-                lefts[count + c] = length - CHUNK * c
+                for ref, value in (
+                    (items, 4 * p + c),
+                    (keys, p + c * CHUNK * n_pass),
+                    (starts, first + 64 * c),
+                    (lefts, length - CHUNK * c),
+                ):
+                    ref.at[pl.ds(c, n_items)][count] = value
             count = count + jnp.right_shift(length + (CHUNK - 1), 5)
         bounds[i // (table_steps // parts)] = jnp.right_shift(count, GROUP_BITS + TURN_BITS)
         return count
@@ -116,9 +119,9 @@
     def gather(group, side):
         code_rows = []
         for n in range(GROUP):
-            item = group * GROUP + n
-            key = keys[item]
-            code_rows.append(codes[pl.ds(starts[item], 8, stride=8), :])
+            at = pl.ds(n, n_items)
+            key = keys.at[at][group * GROUP]
+            code_rows.append(codes[pl.ds(starts.at[at][group * GROUP], 8, stride=8), :])
             for k in range(4):
                 for r in range(8):
                     token = ids.at[pl.ds((4 * r + k) * n_pass, reach)][key]
@@ -147,8 +150,8 @@
     def finish(group, side):
         sums = jnp.dot(squares[side], ones[...], preferred_element_type=jnp.float32)
         for n in range(GROUP):
-            item = group * GROUP + n
-            left = lefts[item]
+            entry = pl.ds(n, n_items)
+            left = lefts.at[entry][group * GROUP]
             embeds = []
             for k in range(4):
                 at = CHUNK * n + 8 * k
@@ -156,7 +159,7 @@
                 embeds.append(raws[side, pl.ds(at, 8), :] * lax.rsqrt(total + 1e-06))
             first = jnp.broadcast_to(embeds[0][0:1, :], (8, DIM))
             embeds = [jnp.where(4 * sub + k < left, embeds[k], first) for k in range(4)]
-            stored[items[item]] = jnp.concatenate(embeds, axis=0).astype(jnp.bfloat16)
+            stored[items.at[entry][group * GROUP]] = jnp.concatenate(embeds, axis=0).astype(jnp.bfloat16)
 
     def body(i, carry):
         for turn in range(TURN):
@@ -234,7 +237,7 @@
     )(lengths, buckets, by_place, tiles, centroids)
 
 
-def score_kernel(rows_per, slots, recv, stored_hbm, out, stored, best, sem):
+def score_kernel(rows_per, recv, stored_hbm, out, stored, best, listed, slots, sem, slots_sem):
     parts = sem.shape[0]
     size = stored.shape[0] // parts
 
@@ -245,6 +248,19 @@
 
     for i in range(parts):
         copy(i).start()
+
+    def read(src, carry):
+        for which in range(2):
+            at = pl.multiple_of(src * rows_per + 64 + 16 * which, 16)
+            meta = recv[pl.ds(at, 16), :].astype(jnp.float32)
+            slot = meta[0:1, :] + 256.0 * meta[8:9, :]
+            listed[pl.ds(2 * src + which, 1), :] = slot.astype(jnp.int32)
+        return carry
+
+    lax.fori_loop(0, recv.shape[0] // rows_per, read, 0)
+    slots_copy = pltpu.make_async_copy(listed, slots, slots_sem)
+    slots_copy.start()
+    slots_copy.wait()
     for i in range(parts):
         copy(i).wait()
 
@@ -257,7 +273,7 @@
         query = 2 * src + which
         sides = [[], []]
         for place in range(16):
-            sides[place % 2].append(stored[slots[query * 16 + place]])
+            sides[place % 2].append(stored[slots[query, place]])
         both = jnp.concatenate([jnp.concatenate(side, axis=0) for side in sides], axis=1)
         sims = lax.dot_general(
             both, pair_q, (((1,), (1,)), ((), ())), preferred_element_type=jnp.float32
@@ -286,12 +302,11 @@
     )
 
 
-def score(rows_per, slots, recv, stored):
+def score(rows_per, recv, stored):
     devices = recv.shape[0] // rows_per
     return pl.pallas_call(
         functools.partial(score_kernel, rows_per),
         in_specs=[
-            pl.BlockSpec(memory_space=pltpu.SMEM),
             pl.BlockSpec(memory_space=pltpu.VMEM),
             pl.BlockSpec(memory_space=pl.ANY),
         ],
@@ -300,12 +315,15 @@
         scratch_shapes=[
             pltpu.VMEM((stored.size // (PTOK * DIM), PTOK, DIM), jnp.bfloat16),
             pltpu.VMEM((2 * devices, 16 * 32), jnp.float32),
+            pltpu.VMEM((2 * devices, DIM), jnp.int32),
+            pltpu.SMEM((2 * devices, DIM), jnp.int32),
             pltpu.SemaphoreType.DMA((16,)),
+            pltpu.SemaphoreType.DMA,
         ],
         compiler_params=pltpu.CompilerParams(vmem_limit_bytes=40 * 2**20),
         cost_estimate=pl.CostEstimate(flops=10**10, bytes_accessed=20 * 2**20, transcendentals=0),
         name="score",
-    )(slots, recv, stored.reshape(-1, PTOK, DIM))
+    )(recv, stored.reshape(-1, PTOK, DIM))
 
 
 def address_kernel(cand, queries, slots, send, dest, seen):
@@ -364,9 +382,7 @@
         send.reshape(devices, SEND_ROWS, DIM), AXES, split_axis=0, concat_axis=0, tiled=True
     )
     stored = unpack(cent_ids, lengths, buckets, codes, centroids)
-    got = recv.reshape(devices, SEND_ROWS // 8, 8, DIM)[:, 8:, 0, :per].astype(jnp.int32)
-    slots = (got[:, 0::2] + 256 * got[:, 1::2]).reshape(-1)
-    scored = score(SEND_ROWS, slots, recv.reshape(devices * SEND_ROWS, DIM), stored)
+    scored = score(SEND_ROWS, recv.reshape(devices * SEND_ROWS, DIM), stored)
     returned = lax.all_to_all(
         scored.reshape(devices, 2, per), AXES, split_axis=0, concat_axis=0, tiled=True
     )

time: 151 us -> 144 us (0.954)
  Pallas kernels: 108 us -> 104 us
  local copies, waits for them, and re-layouts: 9.41 us -> 6.39 us
    slice x2 -> x0, local copies, waits for them, and re-layouts: 2.83 us -> none  [local(): slots = (got[:, 0::2] + 256 * got[:, 1::2]).reshape(-1)]
    pallas_call x1, Pallas kernels: 46.1 us -> 43.4 us  [score(): pl.pallas_call(functools.partial(score_kernel, rows_per), in_specs=[pl.Bl...]
  transfers between devices with their start and end apart: 1 -> 1, of which waited for: 0 -> 0; matrix products, arithmetic and copies ran while one was open for 1% -> 1% of each run, Pallas kernels for 39% -> 41%
where the time goes in v4:
time: 144 us
  Pallas kernels  104 us (72%)
  blocking collectives  21 us (15%)
  starting transfers between devices  11.5 us (8%)
  local copies, waits for them, and re-layouts  6.39 us (4%)
    pallas_call x1, Pallas kernels, unpack(): pl.pallas_call(unpack_kernel, in_specs=[smem] * 2 + [anywhere] * 3, out_s...  58.8 us
    pallas_call x1, Pallas kernels, score(): pl.pallas_call(functools.partial(score_kernel, rows_per), in_specs=[pl.Bl...  43.4 us
    all_to_all x1, blocking collectives, local(): lax.all_to_all(scored.reshape(devices, 2, per), AXES, split_axis=0, conca...  21 us
    all_to_all x1, starting transfers between devices, local(): lax.all_to_all(send.reshape(devices, SEND_ROWS, DIM), AXES, split_axis=0,...  11.5 us
    unnamed x9, local copies, waits for them, and re-layouts  4.63 us
  transfers between devices with their start and end apart: 1, of which 0 were waited for; matrix products, arithmetic and copies ran while one was open for 1% of the time, Pallas kernels for 41%

profile of v4, /device:TPU:1, one launch (start us, length us, event | category | flops | bytes accessed | tf_op | source)
XLA Modules:
  0.0 143.6 jit_solution(11763994333406023587)
XLA Ops:
  0.0 0.0 copy-start.1
  0.0 0.8 copy-done.1
  0.8 0.0 copy-start.2
  0.8 0.7 copy-done.2
  1.5 0.0 copy-start.3
  1.5 0.7 copy-done.3
  2.2 2.2 %address.1 = (bf16[12288,128]{1,0:T(8,128)(2,1)S(1)}, s32[128]{0:T(128)S(1)}) custom-call(s32[8,16]{1,0:T(8,128)S(1)} %copy-done.3, bf16[8,32,128]{2,1,0:T(8,128)(2,1)S(1)} %copy-done.1, s32[8,256]{1,0:T(8,128)S(1)} %copy-done.2), custom_call_target="tpu_custom_call" | custom-call | tf_op jit(solution)/shard_map/address/pallas_call | solution.py:362
  4.5 0.0 copy-start
  4.5 1.6 %copy-done = bf16[12288,128]{1,0:T(8,128)(2,1)} copy-done((bf16[12288,128]{1,0:T(8,128)(2,1)}, bf16[12288,128]{1,0:T(8,128)(2,1)S(1)}, u32[]{:S(2)}) %copy-start) | copy-done | bytes 3145752
  6.1 11.5 %all-to-all-start = ((bf16[128,96,128]{2,1,0:T(8,128)(2,1)}), bf16[128,96,128]{2,1,0:T(8,128)(2,1)S(1)}, u32[]{:S(2)}, u32[]{:S(2)}) async-start(bf16[128,96,128]{2,1,0:T(8,128)(2,1)} %bitcast.15), calls=%async_computation | async-start | bytes 6291456 | tf_op jit(solution)/shard_map/all_to_all | solution.py:381
  17.6 1.1 copy.9
  18.7 0.8 copy.12
  19.5 58.8 %unpack.1 = bf16[2048,32,128]{2,1,0:T(8,128)(2,1)} custom-call(s32[512]{0:T(512)} %lens.1, f32[4]{0:T(128)} %buckets.1, s32[65536]{0:T(1024)} %bitcast.19, s32[16384,128]{1,0:T(8,128)} %bitcast.18, bf16[65536,128]{1,0:T(8,128)(2,1)} %cent.1), custom_call_target="tpu_custom_call" | custom-call | flops 1000000000 | bytes 41943040 | tf_op jit(solution)/shard_map/unpack/pallas_call | solution.py:210
  78.2 0.0 all-to-all-done
  78.2 43.4 %score.1 = f32[256,16]{1,0:T(8,128)S(1)} custom-call(bf16[12288,128]{1,0:T(8,128)(2,1)S(1)} %bitcast.14, bf16[512,128,128]{2,1,0:T(8,128)(2,1)} %bitcast.17), custom_call_target="tpu_custom_call" | custom-call | flops 10000000000 | bytes 20971520 | tf_op jit(solution)/shard_map/score/pallas_call | solution.py:307
  121.7 21.0 %all_to_all.10 = f32[128,2,16]{2,1,0:T(2,128)S(1)} all-to-all(f32[128,2,16]{2,1,0:T(2,128)S(1)} %bitcast.16), channel_id=1, replica_groups=mesh['corpus'=32,'replica'=4] {'corpus','replica'}, dimensions={0} | all-to-all | bytes 32768 | tf_op jit(solution)/shard_map/all_to_all | solution.py:386
  142.6 0.3 fusion
  142.9 0.7 reshape.36
Async XLA Ops:
  0.0 0.8 copy-start.1
  0.8 0.7 copy-start.2
  1.5 0.7 copy-start.3
  4.5 1.6 %copy-start = (bf16[12288,128]{1,0:T(8,128)(2,1)}, bf16[12288,128]{1,0:T(8,128)(2,1)S(1)}, u32[]{:S(2)}) copy-start(bf16[12288,128]{1,0:T(8,128)(2,1)S(1)} %get-tuple-element.8) | copy-start | bytes 9437188
  6.1 72.1 %all-to-all-start = ((bf16[128,96,128]{2,1,0:T(8,128)(2,1)}), bf16[128,96,128]{2,1,0:T(8,128)(2,1)S(1)}, u32[]{:S(2)}, u32[]{:S(2)}) async-start(bf16[128,96,128]{2,1,0:T(8,128)(2,1)} %bitcast.15), calls=%async_computation | async-start | bytes 6291456 | tf_op jit(solution)/shard_map/all_to_all | solution.py:381

commit v5 on v4

--- a/solution.py
+++ b/solution.py
@@ -19,7 +19,7 @@
 TURN = 1 << TURN_BITS
 SCORE_TURN = 16
 GROUP = 1 << GROUP_BITS
-PARTS = 8
+PARTS = 16
 SPARE = 48
 SEND_ROWS = 96
 
@@ -171,11 +171,11 @@
         return carry
 
     def repeat(p, carry):
+        block = stored.at[pl.ds(16 * p, 16)]
         for q in range(4):
-            begin = 4 * (4 * p + q)
-            last = begin + jnp.right_shift(lens[4 * p + q] + (CHUNK - 1), 5) - 1
+            last = jnp.right_shift(lens.at[pl.ds(q, n_pass - 3)][4 * p] + (CHUNK - 1), 5) - 1
             for c in range(1, 4):
-                stored[begin + c] = stored[jnp.minimum(begin + c, last)]
+                block[4 * q + c] = block[4 * q + jnp.minimum(last, c)]
         return carry
 
     def close(j):
@@ -237,7 +237,9 @@
     )(lengths, buckets, by_place, tiles, centroids)
 
 
-def score_kernel(rows_per, recv, stored_hbm, out, stored, best, listed, slots, sem, slots_sem):
+def score_kernel(
+    rows_per, recv_hbm, stored_hbm, out, recv, stored, best, listed, slots, sem, recv_sem, slots_sem
+):
     parts = sem.shape[0]
     size = stored.shape[0] // parts
 
@@ -246,8 +248,11 @@
             stored_hbm.at[pl.ds(i * size, size)], stored.at[pl.ds(i * size, size)], sem.at[i]
         )
 
+    recv_copy = pltpu.make_async_copy(recv_hbm, recv, recv_sem)
+    recv_copy.start()
     for i in range(parts):
         copy(i).start()
+    recv_copy.wait()
 
     def read(src, carry):
         for which in range(2):
@@ -307,17 +312,19 @@
     return pl.pallas_call(
         functools.partial(score_kernel, rows_per),
         in_specs=[
-            pl.BlockSpec(memory_space=pltpu.VMEM),
+            pl.BlockSpec(memory_space=pl.ANY),
             pl.BlockSpec(memory_space=pl.ANY),
         ],
         out_specs=pl.BlockSpec(memory_space=pltpu.VMEM),
         out_shape=jax.ShapeDtypeStruct((2 * devices, 16), jnp.float32),
         scratch_shapes=[
+            pltpu.VMEM(recv.shape, jnp.bfloat16),
             pltpu.VMEM((stored.size // (PTOK * DIM), PTOK, DIM), jnp.bfloat16),
             pltpu.VMEM((2 * devices, 16 * 32), jnp.float32),
             pltpu.VMEM((2 * devices, DIM), jnp.int32),
             pltpu.SMEM((2 * devices, DIM), jnp.int32),
             pltpu.SemaphoreType.DMA((16,)),
+            pltpu.SemaphoreType.DMA,
             pltpu.SemaphoreType.DMA,
         ],
         compiler_params=pltpu.CompilerParams(vmem_limit_bytes=40 * 2**20),

time: 144 us -> 143 us (level)
  no operation moved by 1% of the time
where the time goes in v5:
time: 143 us; the launch traced here: 142 us
  Pallas kernels  104 us (73%)
  blocking collectives  19.6 us (14%)
  starting transfers between devices  11.5 us (8%)
  local copies, waits for them, and re-layouts  6.39 us (4%)
    pallas_call x1, Pallas kernels, unpack(): pl.pallas_call(unpack_kernel, in_specs=[smem] * 2 + [anywhere] * 3, out_s...  58.5 us
    pallas_call x1, Pallas kernels, score(): pl.pallas_call(functools.partial(score_kernel, rows_per), in_specs=[pl.Bl...  43.6 us
    all_to_all x1, blocking collectives, local(): lax.all_to_all(scored.reshape(devices, 2, per), AXES, split_axis=0, conca...  19.6 us
    all_to_all x1, starting transfers between devices, local(): lax.all_to_all(send.reshape(devices, SEND_ROWS, DIM), AXES, split_axis=0,...  11.5 us
    unnamed x9, local copies, waits for them, and re-layouts  4.63 us
  transfers between devices with their start and end apart: 1, of which 0 were waited for; matrix products, arithmetic and copies ran while one was open for 1% of the time, Pallas kernels for 41%

profile of v5, /device:TPU:1, one launch (start us, length us, event | category | flops | bytes accessed | tf_op | source)
XLA Modules:
  0.0 142.2 jit_solution(10698561095724888970)
XLA Ops:
  0.0 0.0 copy-start.1
  0.0 0.8 copy-done.1
  0.8 0.0 copy-start.2
  0.8 0.7 copy-done.2
  1.5 0.0 copy-start.3
  1.5 0.7 copy-done.3
  2.2 2.2 %address.1 = (bf16[12288,128]{1,0:T(8,128)(2,1)S(1)}, s32[128]{0:T(128)S(1)}) custom-call(s32[8,16]{1,0:T(8,128)S(1)} %copy-done.3, bf16[8,32,128]{2,1,0:T(8,128)(2,1)S(1)} %copy-done.1, s32[8,256]{1,0:T(8,128)S(1)} %copy-done.2), custom_call_target="tpu_custom_call" | custom-call | tf_op jit(solution)/shard_map/address/pallas_call | solution.py:369
  4.5 0.0 copy-start
  4.5 1.6 %copy-done = bf16[12288,128]{1,0:T(8,128)(2,1)} copy-done((bf16[12288,128]{1,0:T(8,128)(2,1)}, bf16[12288,128]{1,0:T(8,128)(2,1)S(1)}, u32[]{:S(2)}) %copy-start) | copy-done | bytes 3145752
  6.1 11.5 %all-to-all-start = ((bf16[128,96,128]{2,1,0:T(8,128)(2,1)}), bf16[128,96,128]{2,1,0:T(8,128)(2,1)S(1)}, u32[]{:S(2)}, u32[]{:S(2)}) async-start(bf16[128,96,128]{2,1,0:T(8,128)(2,1)} %bitcast.15), calls=%async_computation | async-start | bytes 6291456 | tf_op jit(solution)/shard_map/all_to_all | solution.py:388
  17.6 1.1 copy.9
  18.7 0.8 copy.12
  19.5 58.5 %unpack.1 = bf16[2048,32,128]{2,1,0:T(8,128)(2,1)} custom-call(s32[512]{0:T(512)} %lens.1, f32[4]{0:T(128)} %buckets.1, s32[65536]{0:T(1024)} %bitcast.19, s32[16384,128]{1,0:T(8,128)} %bitcast.18, bf16[65536,128]{1,0:T(8,128)(2,1)} %cent.1), custom_call_target="tpu_custom_call" | custom-call | flops 1000000000 | bytes 41943040 | tf_op jit(solution)/shard_map/unpack/pallas_call | solution.py:210
  78.0 0.0 all-to-all-done
  78.0 43.6 %score.1 = f32[256,16]{1,0:T(8,128)S(1)} custom-call(bf16[12288,128]{1,0:T(8,128)(2,1)S(1)} %bitcast.14, bf16[512,128,128]{2,1,0:T(8,128)(2,1)} %bitcast.17), custom_call_target="tpu_custom_call" | custom-call | flops 10000000000 | bytes 20971520 | tf_op jit(solution)/shard_map/score/pallas_call | solution.py:312
  121.6 19.6 %all_to_all.10 = f32[128,2,16]{2,1,0:T(2,128)S(1)} all-to-all(f32[128,2,16]{2,1,0:T(2,128)S(1)} %bitcast.16), channel_id=1, replica_groups=mesh['corpus'=32,'replica'=4] {'corpus','replica'}, dimensions={0} | all-to-all | bytes 32768 | tf_op jit(solution)/shard_map/all_to_all | solution.py:393
  141.2 0.3 fusion
  141.5 0.7 reshape.36
Async XLA Ops:
  0.0 0.8 copy-start.1
  0.8 0.7 copy-start.2
  1.5 0.7 copy-start.3
  4.5 1.6 %copy-start = (bf16[12288,128]{1,0:T(8,128)(2,1)}, bf16[12288,128]{1,0:T(8,128)(2,1)S(1)}, u32[]{:S(2)}) copy-start(bf16[12288,128]{1,0:T(8,128)(2,1)S(1)} %get-tuple-element.8) | copy-start | bytes 9437188
  6.1 71.9 %all-to-all-start = ((bf16[128,96,128]{2,1,0:T(8,128)(2,1)}), bf16[128,96,128]{2,1,0:T(8,128)(2,1)S(1)}, u32[]{:S(2)}, u32[]{:S(2)}) async-start(bf16[128,96,128]{2,1,0:T(8,128)(2,1)} %bitcast.15), calls=%async_computation | async-start | bytes 6291456 | tf_op jit(solution)/shard_map/all_to_all | solution.py:388
